TPU v7x, 128 devices: a whole 4x4x4 slice. The times are simulated.
128 devices in a mesh: outer: 32 (over z, y, core), grp: 4 (over x).
Axes of the slice: x: 4, y: 4, z: 4, core: 2. Of those that a mesh axis runs over, the one named last changes fastest.
Arguments:
- link_ids: int32 [98304, 8], P(('outer', 'grp')), may hold values from 0 to 98303, as said below
- path_states: bfloat16 [98304, 8, 128], P(('outer', 'grp')), may hold values from -1 to 1
- final_grad: bfloat16 [98304, 128], P(('outer', 'grp')), may hold values from -6 to 6
- link_states: bfloat16 [98304, 128], P(('outer', 'grp')), may hold values from -6 to 6
- agg_grad: bfloat16 [98304, 128], P(('outer', 'grp')), may hold values from -3 to 3
- w_in: bfloat16 [128, 384], replicated, may hold values from -0.5 to 0.5
- w_rec: bfloat16 [128, 384], replicated, may hold values from -0.5 to 0.5
- b_in: float32 [384], replicated, may hold values from -1 to 1
- b_rec: float32 [384], replicated, may hold values from -1 to 1
Outputs:
- path_grad: bfloat16 [98304, 128], P(('outer', 'grp'))
- link_grad: float32 [98304, 128], P(('outer', 'grp'))
- w_in_grad: float32 [128, 384], replicated
- w_rec_grad: float32 [128, 384], replicated
- b_in_grad: float32 [384], replicated
- b_rec_grad: float32 [384], replicated
Inputs may be any that keep to these rules, and one draw needn't show every extreme that they name: `link_ids`: within the 6144 hops of each device's paths (aligned blocks), at most 72 lie on links of any one owner (owner = id // 768), and exactly 72 for some owner in every block.
All inputs are finite; a program needn't handle non-finite values.
Results may differ from a plain program's by a relative error of at most 0.0035.
Values may be sent and summed in bfloat16 or wider, within the bound.
A program may use at most 128 MiB of HBM per device.

v0:
```python
import math

import jax
import jax.numpy as jnp
from jax import lax
from jax.sharding import PartitionSpec as P


def gru_backward(carry_grad, inputs, states, w_in, w_rec, b_in, b_rec):
    width = states.shape[-1]
    from_input = jnp.dot(inputs, w_in, preferred_element_type=jnp.float32) + b_in
    from_state = jnp.dot(states, w_rec, preferred_element_type=jnp.float32) + b_rec
    update_gate = jax.nn.sigmoid(from_input[:, :width] + from_state[:, :width])
    reset_gate = jax.nn.sigmoid(from_input[:, width : 2 * width] + from_state[:, width : 2 * width])
    recur_part = from_state[:, 2 * width :]
    candidate = jnp.tanh(from_input[:, 2 * width :] + reset_gate * recur_part)
    state_wide = states.astype(jnp.float32)
    cand_pre = carry_grad * (1.0 - update_gate) * (1.0 - candidate * candidate)
    update_pre = carry_grad * (state_wide - candidate) * update_gate * (1.0 - update_gate)
    reset_pre = cand_pre * recur_part * reset_gate * (1.0 - reset_gate)
    input_pre = jnp.concatenate([update_pre, reset_pre, cand_pre], axis=1).astype(jnp.bfloat16)
    state_pre = jnp.concatenate([update_pre, reset_pre, cand_pre * reset_gate], axis=1).astype(
        jnp.bfloat16
    )
    input_grad = jnp.dot(input_pre, w_in.T, preferred_element_type=jnp.float32)
    state_grad = carry_grad * update_gate + jnp.dot(
        state_pre, w_rec.T, preferred_element_type=jnp.float32
    )
    w_in_term = jnp.dot(inputs.T, input_pre, preferred_element_type=jnp.float32)
    w_rec_term = jnp.dot(states.T, state_pre, preferred_element_type=jnp.float32)
    b_in_term = jnp.sum(input_pre.astype(jnp.float32), axis=0)
    b_rec_term = jnp.sum(state_pre.astype(jnp.float32), axis=0)
    return (state_grad, input_grad, w_in_term, w_rec_term, b_in_term, b_rec_term)


def per_device(link_ids, path_states, final_grad, link_states, agg_grad, w_in, w_rec, b_in, b_rec):
    path_count, hop_count = link_ids.shape
    width = link_states.shape[1]
    row_count = path_count * hop_count
    devices = lax.axis_size(("outer", "grp"))
    capacity = 3 * row_count // (2 * devices)
    links_dev = link_states.shape[0]
    flat_ids = jnp.transpose(link_ids).reshape(row_count)
    owners = flat_ids // links_dev
    local_ids = flat_ids - owners * links_dev
    by_owner = jnp.argsort(owners, stable=True)
    sorted_owners = owners[by_owner]
    group_starts = jnp.searchsorted(
        sorted_owners, jnp.arange(devices, dtype=jnp.int32), side="left"
    )
    slot_sorted = (
        sorted_owners * capacity
        + jnp.arange(row_count, dtype=jnp.int32)
        - group_starts[sorted_owners]
    )
    slots = jnp.zeros((row_count,), jnp.int32).at[by_owner].set(slot_sorted)
    requests = jnp.full((devices * capacity,), links_dev, jnp.int32).at[slots].set(local_ids)
    requests = requests.reshape(devices, capacity)
    link_table = jnp.concatenate([link_states, agg_grad], axis=1)
    asked_ids = lax.all_to_all(requests, ("outer", "grp"), split_axis=0, concat_axis=0, tiled=True)
    clipped = jnp.minimum(asked_ids, links_dev - 1)
    returned = lax.all_to_all(
        link_table[clipped], ("outer", "grp"), split_axis=0, concat_axis=0, tiled=True
    )
    fetched = returned.reshape(devices * capacity, 2 * width)[slots].reshape(
        hop_count, path_count, 2 * width
    )
    carry_grad = final_grad.astype(jnp.float32)
    w_in_sum = jnp.zeros(w_in.shape, jnp.float32)
    w_rec_sum = jnp.zeros(w_rec.shape, jnp.float32)
    b_in_sum = jnp.zeros(b_in.shape, jnp.float32)
    b_rec_sum = jnp.zeros(b_rec.shape, jnp.float32)
    hop_grads = [None] * hop_count
    for hop in range(hop_count - 1, -1, -1):
        hop_rows = fetched[hop]
        carry_grad = carry_grad + hop_rows[:, width:].astype(jnp.float32)
        carry_grad, input_grad, w_in_term, w_rec_term, b_in_term, b_rec_term = gru_backward(
            carry_grad, hop_rows[:, :width], path_states[:, hop], w_in, w_rec, b_in, b_rec
        )
        hop_grads[hop] = input_grad
        w_in_sum = w_in_sum + w_in_term
        w_rec_sum = w_rec_sum + w_rec_term
        b_in_sum = b_in_sum + b_in_term
        b_rec_sum = b_rec_sum + b_rec_term
    grad_rows_all = jnp.stack(hop_grads, axis=0).reshape(row_count, width)
    outgoing = jnp.zeros((devices * capacity, width), jnp.float32).at[slots].set(grad_rows_all)
    incoming = lax.all_to_all(
        outgoing.reshape(devices, capacity, width).astype(jnp.bfloat16),
        ("outer", "grp"),
        split_axis=0,
        concat_axis=0,
        tiled=True,
    ).astype(jnp.float32)
    link_grad = (
        jnp.zeros((links_dev, width), jnp.float32)
        .at[asked_ids.reshape(-1)]
        .add(incoming.reshape(devices * capacity, width), mode="drop")
    )
    w_in_all, w_rec_all, b_in_all, b_rec_all = lax.psum(
        (w_in_sum, w_rec_sum, b_in_sum, b_rec_sum), ("outer", "grp")
    )
    norm_scale = 1.0 / math.sqrt(row_count * devices)
    return (
        carry_grad.astype(jnp.bfloat16),
        link_grad,
        w_in_all * norm_scale,
        w_rec_all * norm_scale,
        b_in_all * norm_scale,
        b_rec_all * norm_scale,
    )


def solution(mesh):
    placed = (
        P(("outer", "grp"), None),
        P(("outer", "grp"), None, None),
        P(("outer", "grp"), None),
        P(("outer", "grp"), None),
        P(("outer", "grp"), None),
        P(),
        P(),
        P(),
        P(),
    )
    return jax.shard_map(
        per_device,
        mesh=mesh,
        in_specs=placed,
        out_specs=(P(("outer", "grp"), None), P(("outer", "grp"), None), P(), P(), P(), P()),
        check_vma=False,
    )
```

profile of v0, /device:TPU:1, one launch (start us, length us, event | category | flops | bytes accessed | tf_op | source)
XLA Modules:
  0.0 602.4 jit_solution(14700198796793534372)
XLA Ops:
  8.0 6.7 %sort.17 = (s32[6144]{0:T(1024)}, s32[6144]{0:T(1024)S(1)}) sort(s32[6144]{0:T(1024)S(1)} %get-tuple-element.208, s32[6144]{0:T(1024)S(1)} %iota.10), dimensions={0}, to_apply=%region_0.1 | sort | flops 79872 | bytes 98304 | tf_op jit(solution)/shard_map/jit(argsort)/sort | solution.py:46
  14.8 34.3 %gather_fusion.1 = s32[6144]{0:T(1024)S(1)} fusion(s32[6144]{0:T(1024)S(1)} %get-tuple-element.208, s32[6144]{0:T(1024)S(1)} %get-tuple-element.209), kind=kCustom, calls=%fused_computation.1 | custom fusion | bytes 73728 | tf_op jit(solution)/shard_map/gather | solution.py:47
  49.1 15.8 %while.24 = (s32[]{:T(128)}, u32[128]{0:T(128)S(1)}, u32[128]{0:T(128)S(1)}, s32[6144]{0:T(1024)S(1)}, s32[]{:T(128)}, /*index=5*/s32[]{:T(128)}, s32[]{}) while((s32[]{:T(128)}, u32[128]{0:T(128)S(1)}, u32[128]{0:T(128)S(1)}, s32[6144]{0:T(1024)S(1)}, s32[]{:T(128)}, /*index=5*/s32[]{:T(128)}, s32[]{}) %tuple.107), condition=%wide.region_2.3_spmd.clone, body=%wide.region_1.2_spmd.clone.sunk | while | flops 2692 | bytes 10340 | solution.py:48
  65.0 36.8 %gather_fusion.2 = s32[6144]{0:T(1024)S(1)} fusion(s32[128]{0:T(128)S(1)} %convert_element_type.136, s32[6144]{0:T(1024)S(1)} %broadcast_clamp_fusion.2), kind=kCustom, calls=%fused_computation.2 | custom fusion | bytes 73728 | tf_op jit(solution)/shard_map/gather | solution.py:54
  101.8 23.0 %scatter_custom_fusion = s32[6144]{0:T(1024)S(1)} fusion(s32[6144]{0:T(1024)S(1)} %get-tuple-element.210, s32[6144]{0:T(1024)S(1)} %add_subtract_fusion, s32[]{:T(128)} %constant.53.clone.1), kind=kCustom, calls=%fused_computation.309 | custom fusion | bytes 24580 | tf_op jit(solution)/shard_map/scatter | solution.py:56
  125.4 23.0 %scatter_custom_fusion.1 = s32[9216]{0:T(1024)S(1)} fusion(s32[6144]{0:T(1024)S(1)} %get-tuple-element.206, s32[6144]{0:T(1024)S(1)} %get-tuple-element.207, s32[]{:T(128)} %constant.52.clone.1), kind=kCustom, calls=%fused_computation.304 | custom fusion | bytes 36868 | tf_op jit(solution)/shard_map/scatter | solution.py:57
  149.1 11.5 %all-to-all-start = ((s32[128,1,72]{2,1,0:T(1,128)}), s32[128,1,72]{2,1,0:T(1,128)S(1)}, u32[]{:S(2)}, u32[]{:S(2)}) async-start(s32[128,1,72]{2,1,0:T(1,128)} %bitcast.3), calls=%async_computation | async-start | bytes 131072 | tf_op jit(solution)/shard_map/all_to_all | solution.py:60
  160.7 9.5 %all-to-all-done = s32[128,1,72]{2,1,0:T(1,128)S(1)} async-done(((s32[128,1,72]{2,1,0:T(1,128)}), s32[128,1,72]{2,1,0:T(1,128)S(1)}, u32[]{:S(2)}, u32[]{:S(2)}) %all-to-all-start) | async-done | bytes 36896 | tf_op jit(solution)/shard_map/all_to_all | solution.py:60
  170.8 1.5 fusion.155
  172.4 36.9 %gather_fusion.3 = bf16[9216,256]{1,0:T(8,128)(2,1)} fusion(bf16[768,256]{1,0:T(8,128)(2,1)S(1)} %pad_maximum_fusion.24, s32[9216]{0:T(1024)S(1)} %broadcast_clamp_fusion), kind=kCustom, calls=%fused_computation.3 | custom fusion | bytes 9474048 | tf_op jit(solution)/shard_map/gather | solution.py:63
  209.3 6.0 all-to-all-start.1
  215.3 3.3 fusion.154
  224.5 1.4 convolution_add_fusion.14
  225.9 1.4 convolution_add_fusion.12
  227.3 1.4 convolution_add_fusion.10
  228.7 1.4 convolution_add_fusion.8
  230.0 1.4 convolution_add_fusion.6
  232.8 1.4 convolution_add_fusion.2
  234.2 1.4 convolution_add_fusion
  236.4 37.7 %all-to-all-done.1 = bf16[128,72,256]{2,1,0:T(8,128)(2,1)} async-done(((bf16[128,72,256]{2,1,0:T(8,128)(2,1)}), bf16[128,72,256]{2,1,0:T(8,128)(2,1)}, u32[]{:S(2)}, u32[]{:S(2)}) %all-to-all-start.1) | async-done | bytes 4718624 | tf_op jit(solution)/shard_map/all_to_all | solution.py:62
  274.1 25.2 %gather_fusion.4 = bf16[6144,256]{1,0:T(8,128)(2,1)S(1)} fusion(bf16[9216,256]{1,0:T(8,128)(2,1)} %bitcast.6, s32[6144]{0:T(1024)} %get-tuple-element.205), kind=kCustom, calls=%fused_computation.4 | custom fusion | bytes 6316032 | tf_op jit(solution)/shard_map/gather | solution.py:65
  300.6 1.4 convolution_add_fusion.15
  302.0 1.5 convolution_add_fusion.13
  303.4 1.4 convolution_add_fusion.11
  304.9 1.4 convolution_add_fusion.9
  306.3 1.4 convolution_add_fusion.7
  307.7 1.4 convolution_add_fusion.5
  309.1 1.4 convolution_add_fusion.3
  311.9 1.7 copy.106
  313.6 1.7 copy.108
  315.3 1.8 copy.110
  317.1 1.8 copy.112
  318.8 1.7 copy.114
  320.6 1.7 copy.116
  322.3 1.7 copy.118
  324.1 1.7 copy.120
  325.8 2.1 fusion.137
  355.6 1.7 copy-done.120
  357.3 18.5 %scatter_custom_fusion.2 = f32[9216,128]{1,0:T(8,128)} fusion(s32[6144]{0:T(1024)} %copy-done.119, f32[6144,128]{1,0:T(8,128)} %bitcast.135, f32[]{:T(128)} %constant.64.clone.1), kind=kCustom, calls=%fused_computation.19 | custom fusion | bytes 4719104 | tf_op jit(solution)/shard_map/scatter | solution.py:86
  375.8 3.5 convert_element_type.154
  379.3 5.2 all-to-all-start.2
  384.6 1.7 copy.96
  386.4 1.5 convolution_add_fusion.34
  391.3 1.6 convert_reduce_fusion.6
  395.5 74.0 %all-reduce = (f32[384]{0:T(512)S(1)}, f32[384]{0:T(512)S(1)}) all-reduce(f32[384]{0:T(512)S(1)} %get-tuple-element.221, f32[384]{0:T(512)S(1)} %get-tuple-element.220), channel_id=1, replica_groups=mesh['outer'=32,'grp'=4] {'outer','grp'}, use_global_device_ids=true, to_apply=%region_17.18 | all-reduce | flops 768 | bytes 6144 | tf_op jit(solution)/shard_map/psum | solution.py:99
  470.6 72.1 %all-reduce.4.cloned.1.call-done = (f32[128,384]{1,0:T(8,128)}, f32[128,384]{1,0:T(8,128)}) async-done(((f32[128,384]{1,0:T(8,128)}, f32[128,384]{1,0:T(8,128)}), (f32[128,384]{1,0:T(8,128)}, f32[128,384]{1,0:T(8,128)})) %all-reduce.4.cloned.1.call-update) | async-done | bytes 393232 | tf_op jit(solution)/shard_map/psum | solution.py:99
  542.8 1.8 broadcast_multiply_fusion
  544.6 50.7 %scatter_custom_fusion.3 = f32[768,128]{1,0:T(8,128)} fusion(s32[9216]{0:T(1024)} %bitcast.133, bf16[9216,128]{1,0:T(8,128)(2,1)} %bitcast.28, f32[]{:T(128)} %constant.64.clone.1), kind=kCustom, calls=%fused_computation.17 | custom fusion | flops 2359296 | bytes 2753024 | tf_op jit(solution)/shard_map/scatter-add | solution.py:97
  (376 shorter events, 62.4 us)
Async XLA Ops:
  7.2 293.4 %copy-start = (bf16[128,384]{1,0:T(8,128)(2,1)S(1)}, bf16[128,384]{1,0:T(8,128)(2,1)}, u32[]{:S(2)}) copy-start(bf16[128,384]{1,0:T(8,128)(2,1)} %param.16) | copy-start | bytes 294916
  64.9 95.7 %copy-start.99 = (bf16[768,128]{1,0:T(8,128)(2,1)S(1)}, bf16[768,128]{1,0:T(8,128)(2,1)}, u32[]{:S(2)}) copy-start(bf16[768,128]{1,0:T(8,128)(2,1)} %param.15) | copy-start | bytes 589828
  65.0 95.7 %copy-start.100 = (bf16[768,128]{1,0:T(8,128)(2,1)S(1)}, bf16[768,128]{1,0:T(8,128)(2,1)}, u32[]{:S(2)}) copy-start(bf16[768,128]{1,0:T(8,128)(2,1)} %param.14) | copy-start | bytes 589828
  125.4 23.7 %copy-start.119 = (s32[6144]{0:T(1024)}, s32[6144]{0:T(1024)S(1)}, u32[]{:S(2)}) copy-start(s32[6144]{0:T(1024)S(1)} %get-tuple-element.206) | copy-start | bytes 73732
  149.1 21.1 %all-to-all-start = ((s32[128,1,72]{2,1,0:T(1,128)}), s32[128,1,72]{2,1,0:T(1,128)S(1)}, u32[]{:S(2)}, u32[]{:S(2)}) async-start(s32[128,1,72]{2,1,0:T(1,128)} %bitcast.3), calls=%async_computation | async-start | bytes 131072 | tf_op jit(solution)/shard_map/all_to_all | solution.py:60
  209.3 6.0 copy-start.4
  209.3 64.8 %all-to-all-start.1 = ((bf16[128,72,256]{2,1,0:T(8,128)(2,1)}), bf16[128,72,256]{2,1,0:T(8,128)(2,1)}, u32[]{:S(2)}, u32[]{:S(2)}) async-start(bf16[128,72,256]{2,1,0:T(8,128)(2,1)} %bitcast.129), calls=%async_computation.1 | async-start | bytes 9437184 | tf_op jit(solution)/shard_map/all_to_all | solution.py:62
  218.6 3.7 copy-start.37
  218.6 4.0 copy-start.36
  219.9 4.6 copy-start.34
  222.3 3.6 copy-start.32
  222.6 4.6 copy-start.30
  223.0 5.7 copy-start.28
  223.4 6.7 %copy-start.26 = (bf16[768,1,128]{0,2,1:T(8,128)(2,1)}, bf16[768,1,128]{0,2,1:T(8,128)(2,1)S(1)}, u32[]{:S(2)}) copy-start(bf16[768,1,128]{0,2,1:T(8,128)(2,1)S(1)} %copy.115) | copy-start | bytes 589828
  223.7 7.7 %copy-start.24 = (bf16[768,1,128]{0,2,1:T(8,128)(2,1)}, bf16[768,1,128]{0,2,1:T(8,128)(2,1)S(1)}, u32[]{:S(2)}) copy-start(bf16[768,1,128]{0,2,1:T(8,128)(2,1)S(1)} %copy.117) | copy-start | bytes 589828
  224.1 8.7 %copy-start.22 = (bf16[768,1,128]{0,2,1:T(8,128)(2,1)}, bf16[768,1,128]{0,2,1:T(8,128)(2,1)S(1)}, u32[]{:S(2)}) copy-start(bf16[768,1,128]{0,2,1:T(8,128)(2,1)S(1)} %copy.119) | copy-start | bytes 589828
  224.5 9.8 %copy-start.20 = (bf16[768,1,128]{0,2,1:T(8,128)(2,1)}, bf16[768,1,128]{0,2,1:T(8,128)(2,1)S(1)}, u32[]{:S(2)}) copy-start(bf16[768,1,128]{0,2,1:T(8,128)(2,1)S(1)} %copy.121) | copy-start | bytes 589828
  232.8 2.8 copy-start.91
  325.8 2.4 copy-start.2
  325.8 2.4 copy-start.19
  325.8 2.5 copy-start.35
  327.9 27.3 %copy-start.38 = (bf16[768,128]{0,1:T(8,128)(2,1)}, bf16[768,128]{0,1:T(8,128)(2,1)S(1)}, u32[]{:S(2)}) copy-start(bf16[768,128]{0,1:T(8,128)(2,1)S(1)} %get-tuple-element.137) | copy-start | bytes 589828
  328.6 2.6 copy-start.44
  328.6 26.6 %copy-start.40 = (bf16[768,128]{0,1:T(8,128)(2,1)}, bf16[768,128]{0,1:T(8,128)(2,1)S(1)}, u32[]{:S(2)}) copy-start(bf16[768,128]{0,1:T(8,128)(2,1)S(1)} %get-tuple-element.193) | copy-start | bytes 589828
  328.6 26.6 %copy-start.42 = (bf16[768,128]{0,1:T(8,128)(2,1)}, bf16[768,128]{0,1:T(8,128)(2,1)S(1)}, u32[]{:S(2)}) copy-start(bf16[768,128]{0,1:T(8,128)(2,1)S(1)} %get-tuple-element.194) | copy-start | bytes 589828
  331.2 23.6 %copy-start.101 = (bf16[768,128]{0,1:T(8,128)(2,1)}, bf16[768,128]{0,1:T(8,128)(2,1)S(1)}, u32[]{:S(2)}) copy-start(bf16[768,128]{0,1:T(8,128)(2,1)S(1)} %get-tuple-element.140) | copy-start | bytes 589828
  331.5 23.3 %copy-start.46 = (bf16[768,128]{0,1:T(8,128)(2,1)}, bf16[768,128]{0,1:T(8,128)(2,1)S(1)}, u32[]{:S(2)}) copy-start(bf16[768,128]{0,1:T(8,128)(2,1)S(1)} %get-tuple-element.191) | copy-start | bytes 589828
  331.5 23.3 %copy-start.47 = (bf16[768,128]{0,1:T(8,128)(2,1)}, bf16[768,128]{0,1:T(8,128)(2,1)S(1)}, u32[]{:S(2)}) copy-start(bf16[768,128]{0,1:T(8,128)(2,1)S(1)} %get-tuple-element.192) | copy-start | bytes 589828
  333.6 20.7 %copy-start.102 = (bf16[768,128]{0,1:T(8,128)(2,1)}, bf16[768,128]{0,1:T(8,128)(2,1)S(1)}, u32[]{:S(2)}) copy-start(bf16[768,128]{0,1:T(8,128)(2,1)S(1)} %get-tuple-element.143) | copy-start | bytes 589828
  334.3 20.0 %copy-start.49 = (bf16[768,128]{0,1:T(8,128)(2,1)}, bf16[768,128]{0,1:T(8,128)(2,1)S(1)}, u32[]{:S(2)}) copy-start(bf16[768,128]{0,1:T(8,128)(2,1)S(1)} %get-tuple-element.189) | copy-start | bytes 589828
  334.3 20.0 %copy-start.51 = (bf16[768,128]{0,1:T(8,128)(2,1)}, bf16[768,128]{0,1:T(8,128)(2,1)S(1)}, u32[]{:S(2)}) copy-start(bf16[768,128]{0,1:T(8,128)(2,1)S(1)} %get-tuple-element.190) | copy-start | bytes 589828
  336.4 17.5 %copy-start.104 = (bf16[768,128]{0,1:T(8,128)(2,1)}, bf16[768,128]{0,1:T(8,128)(2,1)S(1)}, u32[]{:S(2)}) copy-start(bf16[768,128]{0,1:T(8,128)(2,1)S(1)} %get-tuple-element.146) | copy-start | bytes 589828
  337.1 16.8 %copy-start.55 = (bf16[768,128]{0,1:T(8,128)(2,1)}, bf16[768,128]{0,1:T(8,128)(2,1)S(1)}, u32[]{:S(2)}) copy-start(bf16[768,128]{0,1:T(8,128)(2,1)S(1)} %get-tuple-element.187) | copy-start | bytes 589828
  337.1 16.8 %copy-start.57 = (bf16[768,128]{0,1:T(8,128)(2,1)}, bf16[768,128]{0,1:T(8,128)(2,1)S(1)}, u32[]{:S(2)}) copy-start(bf16[768,128]{0,1:T(8,128)(2,1)S(1)} %get-tuple-element.188) | copy-start | bytes 589828
  339.2 14.3 %copy-start.106 = (bf16[768,128]{0,1:T(8,128)(2,1)}, bf16[768,128]{0,1:T(8,128)(2,1)S(1)}, u32[]{:S(2)}) copy-start(bf16[768,128]{0,1:T(8,128)(2,1)S(1)} %get-tuple-element.149) | copy-start | bytes 589828
  339.9 13.6 %copy-start.63 = (bf16[768,128]{0,1:T(8,128)(2,1)}, bf16[768,128]{0,1:T(8,128)(2,1)S(1)}, u32[]{:S(2)}) copy-start(bf16[768,128]{0,1:T(8,128)(2,1)S(1)} %get-tuple-element.186) | copy-start | bytes 589828
  339.9 46.4 %copy-start.61 = (bf16[768,128]{0,1:T(8,128)(2,1)}, bf16[768,128]{0,1:T(8,128)(2,1)S(1)}, u32[]{:S(2)}) copy-start(bf16[768,128]{0,1:T(8,128)(2,1)S(1)} %get-tuple-element.185) | copy-start | bytes 589828
  342.1 11.1 %copy-start.108 = (bf16[768,128]{0,1:T(8,128)(2,1)}, bf16[768,128]{0,1:T(8,128)(2,1)S(1)}, u32[]{:S(2)}) copy-start(bf16[768,128]{0,1:T(8,128)(2,1)S(1)} %get-tuple-element.152) | copy-start | bytes 589828
  342.7 10.4 %copy-start.67 = (bf16[768,128]{0,1:T(8,128)(2,1)}, bf16[768,128]{0,1:T(8,128)(2,1)S(1)}, u32[]{:S(2)}) copy-start(bf16[768,128]{0,1:T(8,128)(2,1)S(1)} %get-tuple-element.183) | copy-start | bytes 589828
  342.8 10.4 %copy-start.70 = (bf16[768,128]{0,1:T(8,128)(2,1)}, bf16[768,128]{0,1:T(8,128)(2,1)S(1)}, u32[]{:S(2)}) copy-start(bf16[768,128]{0,1:T(8,128)(2,1)S(1)} %get-tuple-element.184) | copy-start | bytes 589828
  344.9 7.9 %copy-start.111 = (bf16[768,128]{0,1:T(8,128)(2,1)}, bf16[768,128]{0,1:T(8,128)(2,1)S(1)}, u32[]{:S(2)}) copy-start(bf16[768,128]{0,1:T(8,128)(2,1)S(1)} %get-tuple-element.155) | copy-start | bytes 589828
  345.6 7.2 %copy-start.75 = (bf16[768,128]{0,1:T(8,128)(2,1)}, bf16[768,128]{0,1:T(8,128)(2,1)S(1)}, u32[]{:S(2)}) copy-start(bf16[768,128]{0,1:T(8,128)(2,1)S(1)} %get-tuple-element.181) | copy-start | bytes 589828
  345.6 7.2 %copy-start.78 = (bf16[768,128]{0,1:T(8,128)(2,1)}, bf16[768,128]{0,1:T(8,128)(2,1)S(1)}, u32[]{:S(2)}) copy-start(bf16[768,128]{0,1:T(8,128)(2,1)S(1)} %get-tuple-element.182) | copy-start | bytes 589828
  347.7 3.0 copy-start.114
  348.4 2.3 copy-start.83
  379.3 165.2 %all-to-all-start.2 = ((bf16[128,72,128]{2,1,0:T(8,128)(2,1)}), bf16[128,72,128]{2,1,0:T(8,128)(2,1)}, u32[]{:S(2)}, u32[]{:S(2)}) async-start(bf16[128,72,128]{2,1,0:T(8,128)(2,1)} %bitcast.130), calls=%async_computation.2 | async-start | bytes 4718592 | tf_op jit(solution)/shard_map/all_to_all | solution.py:87
  384.6 158.2 %all-reduce.4.cloned.1.call-start = ((), (), s32[]{:S(2)}) async-start(), calls=%async_computation.3 | async-start | bytes 786432 | tf_op jit(solution)/shard_map/psum | solution.py:99
  390.2 2.7 copy-start.39
  (77 other events, 112.3 us)
Sparse Core Ops, SparseCore 0:
  391.4 151.3 all-reduce.3
where the time goes:
time: 610 us; the launch traced here: 602 us
  local copies, waits for them, and re-layouts  257 us (42%)
  waiting for transfers between devices  119 us (20%)
  other arithmetic  74.6 us (12%)
  blocking collectives  74 us (12%)
  matrix products  38.7 us (6%)
  starting transfers between devices  22.7 us (4%)
  between operations  15.9 us (3%)
    psum x1, blocking collectives, per_device(): lax.psum((w_in_sum, w_rec_sum, b_in_sum, b_rec_sum), ('outer', 'grp'))  74 us
    psum x1, waiting for transfers between devices, per_device(): lax.psum((w_in_sum, w_rec_sum, b_in_sum, b_rec_sum), ('outer', 'grp'))  72.1 us
    scatter-add x1, other arithmetic, per_device(): link_grad = jnp.zeros((links_dev, width), jnp.float32).at[asked_ids.resha...  50.7 us
    all_to_all x1, waiting for transfers between devices, per_device(): lax.all_to_all(link_table[clipped], ('outer', 'grp'), split_axis=0, conca...  37.7 us
    unnamed x260, local copies, waits for them, and re-layouts  37.2 us
    gather x1, local copies, waits for them, and re-layouts, per_device(): link_table[clipped]  36.9 us
    gather x1, local copies, waits for them, and re-layouts, per_device(): group_starts[sorted_owners]  36.8 us
    gather x1, local copies, waits for them, and re-layouts, per_device(): sorted_owners = owners[by_owner]  34.3 us
  transfers between devices with their start and end apart: 4, of which 3 were waited for; matrix products, arithmetic and copies ran while one was open for 5% of the time, Pallas kernels for 0%

commit v1 on v0

v1 whole, which is shorter than its diff:
```python
import functools
import math

import jax
import jax.numpy as jnp
from jax import lax
from jax.experimental import pallas as pl
from jax.experimental.pallas import tpu as pltpu
from jax.sharding import PartitionSpec as P

MESH = pl.DeviceIdType.MESH
F32 = jnp.float32
BF16 = jnp.bfloat16
I32 = jnp.int32

OUTER = 32
GRP = 4
DEV = OUTER * GRP
HOPS = 8
PATHS = 768
LINKS = 768
WIDTH = 128
ROWS = PATHS * HOPS
CAP = 3 * ROWS // (2 * DEV)
STRIDE = 11
CHUNK = 256
NT = (((1,), (1,)), ((), ()))
TN = (((0,), (0,)), ((), ()))


def iota(shape, dim):
    return lax.broadcasted_iota(I32, shape, dim)


def kernel(
    ids_ref, states_ref, final_ref, link_ref, agg_ref, w_in_ref, w_rec_ref, b_in_ref, b_rec_ref,
    path_out, link_out, w_in_out, w_rec_out, bias_out,
    upper, owner_v, slot_v, asks, ask_send, ask_recv, ask_cols, pos_v, slot_s, pos_s, table,
    x_send, agg_send, x_recv, agg_recv, out_send, out_recv, rows_f, states_f, stage,
    coef_a, coef_b, coef_g, coef_r, coef_u, x_b, h_b, carry, w_part, w_recv, w_total, w_all, bias_acc,
    ask_ss, ask_rs, x_ss, x_rs, agg_ss, agg_rs, out_ss, out_rs, w1_ss, w1_rs, w2_ss, w2_rs, local_s,
):
    me_o = lax.axis_index("outer")
    me_g = lax.axis_index("grp")
    me = me_o * GRP + me_g

    def ahead(k):
        o = lax.rem(me_o + lax.rem((k // GRP) * STRIDE, OUTER), OUTER)
        g = lax.rem(me_g + lax.rem(k, GRP), GRP)
        return o, g, o * GRP + g

    def behind(k):
        o = lax.rem(me_o + OUTER - lax.rem((k // GRP) * STRIDE, OUTER), OUTER)
        g = lax.rem(me_g + GRP - lax.rem(k, GRP), GRP)
        return o * GRP + g

    def send(src, dst, send_sem, recv_sem, k):
        o, g, p = ahead(k)
        return pltpu.make_async_remote_copy(
            src_ref=src(p), dst_ref=dst, send_sem=send_sem.at[p], recv_sem=recv_sem.at[me],
            device_id=(o, g), device_id_type=MESH,
        )

    def arrived(dst, recv_sem, p):
        pltpu.make_async_copy(dst, dst, recv_sem.at[p]).wait()

    barrier = pltpu.get_barrier_semaphore()

    def greet(k, _):
        o, g, _p = ahead(k)
        pl.semaphore_signal(barrier, inc=1, device_id=(o, g), device_id_type=MESH)
        return 0

    lax.fori_loop(1, DEV, greet, 0)

    def upper_block(b, _):
        r = pl.multiple_of(b * 128, 128)
        upper[pl.ds(r, 128), :] = jnp.where(
            iota((128, PATHS), 0) + r < iota((128, PATHS), 1), 1.0, 0.0
        ).astype(BF16)
        return 0

    lax.fori_loop(0, PATHS // 128, upper_block, 0)
    owner_v[...] = ((ids_ref[...] >> 8) * 171) >> 9
    asks[...] = jnp.zeros_like(asks)

    def index_hop(t, base):
        own = owner_v[pl.ds(t, 1), :]
        local = ids_ref[pl.ds(t, 1), :] - own * LINKS + 1
        hot = iota((DEV, PATHS), 0) == own
        hot_b = jnp.where(hot, 1.0, 0.0).astype(BF16)
        before = jnp.dot(hot_b, upper[...], preferred_element_type=F32) + base
        rank = jnp.sum(jnp.where(hot, before, 0.0), axis=0, keepdims=True).astype(I32)
        slot_v[pl.ds(t, 1), :] = jnp.clip(own * CAP + rank, 0, DEV * CAP - 1)
        at_rank = iota((128, PATHS), 0) == rank
        pos = iota((1, PATHS), 1) + t * PATHS

        def parts(row, bits):
            high = (row >> bits).astype(F32)
            low = (row & ((1 << bits) - 1)).astype(F32)
            both = jnp.concatenate(
                [jnp.where(at_rank, high, 0.0), jnp.where(at_rank, low, 0.0)], axis=0
            ).astype(BF16)
            return lax.dot_general(hot_b, both, NT, preferred_element_type=F32)

        asks[:, :256] += parts(local, 5)
        asks[:, 256:] += parts(pos, 7)
        return base + jnp.sum(jnp.where(hot, 1.0, 0.0), axis=1, keepdims=True)

    lax.fori_loop(0, HOPS, index_hop, jnp.zeros((DEV, 1), F32))
    w_all[:DEV, :] = asks[:, :128] * 32.0 + asks[:, 128:256]
    pos_v[...] = jnp.clip((asks[:, 256:384] * 128.0 + asks[:, 384:]).astype(I32), 0, ROWS - 1)
    to_slots = pltpu.make_async_copy(slot_v, slot_s, local_s.at[0])
    to_pos = pltpu.make_async_copy(pos_v, pos_s, local_s.at[1])
    to_slots.start()
    to_pos.start()

    def spread(o, _):
        ask_send[o] = w_all[pl.ds(o, 1), :].astype(I32)
        return 0

    lax.fori_loop(0, DEV, spread, 0)
    ask_recv[me] = ask_send[me]
    pl.semaphore_wait(barrier, DEV - 1)

    def ask_copy(k):
        return send(lambda p: ask_send.at[p], ask_recv.at[me], ask_ss, ask_rs, k)

    def start_ask(k, _):
        ask_copy(k).start()
        return 0

    lax.fori_loop(1, DEV, start_ask, 0)

    table[:, :WIDTH] = link_ref[...]
    table[:, WIDTH:] = agg_ref[...]

    def widen(b, _):
        r = pl.multiple_of(b * 64, 64)
        block = states_ref[pl.ds(r, 64)].astype(F32)
        states_f[pl.ds(pl.multiple_of(b * 512, 512), 512), :] = block.reshape(512, WIDTH)
        return 0

    lax.fori_loop(0, PATHS // 64, widen, 0)
    carry[...] = final_ref[...].astype(F32)
    to_slots.wait()
    to_pos.wait()

    def wait_ask(k, _):
        p = behind(k)
        arrived(ask_recv.at[p], ask_rs, p)
        return 0

    lax.fori_loop(1, DEV, wait_ask, 0)
    ask_cols[...] = jnp.transpose((ask_recv[...].reshape(DEV, 128) - 1).astype(F32))

    def x_copy(k):
        return send(lambda p: x_send.at[p], x_recv.at[me], x_ss, x_rs, k)

    def agg_copy(k):
        return send(lambda p: agg_send.at[p], agg_recv.at[me], agg_ss, agg_rs, k)

    def answer(i, _):
        o = lax.rem(me_o + lax.rem(i * STRIDE, OUTER), OUTER)
        cols = []
        for g in range(GRP):
            mine = jnp.where(iota((CAP, 128), 1) == o * GRP + g, ask_cols[:CAP, :], 0.0)
            cols.append(jnp.sum(mine, axis=1, keepdims=True))
        col = jnp.concatenate(cols, axis=0).astype(I32)
        hot = jnp.where(iota((GRP * CAP, LINKS), 1) == col, 1.0, 0.0).astype(BF16)
        got = jnp.dot(hot, table[...], preferred_element_type=F32)
        for g in range(GRP):
            x_send[o * GRP + g] = got[g * CAP : (g + 1) * CAP, :WIDTH].astype(BF16)
            agg_send[o * GRP + g] = got[g * CAP : (g + 1) * CAP, WIDTH:].astype(BF16)
        for g in range(GRP):
            if g == 0:
                @pl.when(i > 0)
                def _():
                    x_copy(i * GRP).start()
            else:
                x_copy(i * GRP + g).start()
        return 0

    lax.fori_loop(0, OUTER, answer, 0)

    def start_agg(k, _):
        agg_copy(k).start()
        return 0

    lax.fori_loop(1, DEV, start_agg, 0)
    x_recv[me] = x_send[me]
    agg_recv[me] = agg_send[me]

    def take(recv, recv_sem):
        def body(k, _):
            p = behind(k)

            @pl.when(k > 0)
            def _():
                arrived(recv.at[p], recv_sem, p)

            rows_f[pl.ds(pl.multiple_of(p * CAP, 8), CAP), :] = recv[p].astype(F32)
            return 0

        lax.fori_loop(0, DEV, body, 0)

    def to_path_order(t):
        def body(b, _):
            r = pl.multiple_of(b * 16, 16)
            for j in range(16):
                stage[pl.ds(r + j, 1), :] = rows_f[pl.ds(slot_s[t, r + j], 1), :]
            return 0

        lax.fori_loop(0, PATHS // 16, body, 0)

    take(x_recv, x_rs)

    def forward_hop(t, _):
        to_path_order(t)

        def chunk(c, _):
            r = pl.multiple_of(c * CHUNK, CHUNK)
            out = pl.ds(pl.multiple_of(t * PATHS + r, CHUNK), CHUNK)
            x = stage[pl.ds(r, CHUNK), :].astype(BF16)
            h = states_f[pl.ds(r * HOPS + t, CHUNK, stride=HOPS), :]
            hb = h.astype(BF16)
            x_b[out, :] = x
            h_b[out, :] = hb
            gx = jnp.dot(x, w_in_ref[...], preferred_element_type=F32) + b_in_ref[...]
            gh = jnp.dot(hb, w_rec_ref[...], preferred_element_type=F32) + b_rec_ref[...]
            u = jax.nn.sigmoid(gx[:, :WIDTH] + gh[:, :WIDTH])
            r_gate = jax.nn.sigmoid(gx[:, WIDTH : 2 * WIDTH] + gh[:, WIDTH : 2 * WIDTH])
            recur = gh[:, 2 * WIDTH :]
            cand = jnp.tanh(gx[:, 2 * WIDTH :] + r_gate * recur)
            coef_a[out, :] = (1.0 - u) * (1.0 - cand * cand)
            coef_b[out, :] = (h - cand) * u * (1.0 - u)
            coef_g[out, :] = recur * r_gate * (1.0 - r_gate)
            coef_r[out, :] = r_gate
            coef_u[out, :] = u
            return 0

        lax.fori_loop(0, PATHS // CHUNK, chunk, 0)
        return 0

    lax.fori_loop(0, HOPS, forward_hop, 0)
    take(agg_recv, agg_rs)
    w_in_out[...] = jnp.zeros_like(w_in_out)
    w_rec_out[...] = jnp.zeros_like(w_rec_out)
    bias_acc[...] = jnp.zeros_like(bias_acc)
    grads = coef_a

    def backward_hop(i, _):
        t = HOPS - 1 - i
        to_path_order(t)

        def chunk(c, _):
            r = pl.multiple_of(c * CHUNK, CHUNK)
            here = pl.ds(r, CHUNK)
            out = pl.ds(pl.multiple_of(t * PATHS + r, CHUNK), CHUNK)
            cg = carry[here, :] + stage[here, :]
            pc = cg * coef_a[out, :]
            pu = (cg * coef_b[out, :]).astype(BF16)
            pr = (pc * coef_g[out, :]).astype(BF16)
            pcr = (pc * coef_r[out, :]).astype(BF16)
            in_pre = jnp.concatenate([pu, pr, pc.astype(BF16)], axis=1)
            st_pre = jnp.concatenate([pu, pr, pcr], axis=1)
            carry[here, :] = cg * coef_u[out, :] + lax.dot_general(
                st_pre, w_rec_ref[...], NT, preferred_element_type=F32
            )
            grads[out, :] = lax.dot_general(in_pre, w_in_ref[...], NT, preferred_element_type=F32)
            w_in_out[...] += lax.dot_general(x_b[out, :], in_pre, TN, preferred_element_type=F32)
            w_rec_out[...] += lax.dot_general(h_b[out, :], st_pre, TN, preferred_element_type=F32)
            bias_acc[0:1, :] += jnp.sum(in_pre.astype(F32), axis=0, keepdims=True)
            bias_acc[1:2, :] += jnp.sum(st_pre.astype(F32), axis=0, keepdims=True)
            return 0

        lax.fori_loop(0, PATHS // CHUNK, chunk, 0)
        return 0

    lax.fori_loop(0, HOPS, backward_hop, 0)
    path_out[...] = carry[...].astype(BF16)

    for r in range(3):
        lanes = slice(r * WIDTH, (r + 1) * WIDTH)
        w_part[pl.ds(r, DEV, stride=8), :] = w_in_out[:, lanes]
        w_part[pl.ds(3 + r, DEV, stride=8), :] = w_rec_out[:, lanes]
    bias8 = jnp.concatenate(
        [bias_acc[0:1, r * WIDTH : (r + 1) * WIDTH] for r in range(3)]
        + [bias_acc[1:2, r * WIDTH : (r + 1) * WIDTH] for r in range(3)]
        + [jnp.zeros((2, WIDTH), F32)],
        axis=0,
    )
    w_part[pl.ds(6, DEV, stride=8), :] = jnp.concatenate([bias8] * (DEV // 8), axis=0)
    w_part[pl.ds(7, DEV, stride=8), :] = jnp.zeros((DEV, WIDTH), F32)

    def rows8(ref, p):
        return ref.at[pl.ds(pl.multiple_of(p * 8, 8), 8), :]

    def part_copy(k):
        return send(lambda p: rows8(w_part, p), rows8(w_recv, me), w1_ss, w1_rs, k)

    def start_part(k, _):
        part_copy(k).start()
        return 0

    lax.fori_loop(1, DEV, start_part, 0)

    def out_copy(k):
        return send(lambda p: out_send.at[p], out_recv.at[me], out_ss, out_rs, k)

    def give(k, _):
        _o, _g, p = ahead(k)
        for j in range(CAP):
            stage[pl.ds(j, 1), :] = grads[pl.ds(pos_s[p, j], 1), :]
        out_send[p] = stage[:CAP, :].astype(BF16)

        @pl.when(k > 0)
        def _():
            out_copy(k).start()

        return 0

    lax.fori_loop(0, DEV, give, 0)
    out_recv[me] = out_send[me]

    own_rows = pl.ds(pl.multiple_of(me * 8, 8), 8)

    def add_part(k, total):
        p = behind(k)
        arrived(rows8(w_recv, p), w1_rs, p)
        return total + w_recv[pl.ds(pl.multiple_of(p * 8, 8), 8), :]

    total = lax.fori_loop(1, DEV, add_part, w_part[own_rows, :]) * (1.0 / math.sqrt(ROWS * DEV))
    w_total[...] = total

    def total_copy(k):
        return send(lambda p: w_total, rows8(w_all, me), w2_ss, w2_rs, k)

    def start_total(k, _):
        total_copy(k).start()
        return 0

    lax.fori_loop(1, DEV, start_total, 0)
    w_all[own_rows, :] = total

    link_out[...] = jnp.zeros_like(link_out)

    def collect(k, _):
        p = behind(k)

        @pl.when(k > 0)
        def _():
            arrived(out_recv.at[p], out_rs, p)

        hot = jnp.where(iota((LINKS, 128), 0) == ask_recv[p] - 1, 1.0, 0.0).astype(BF16)
        link_out[...] += jnp.dot(hot[:, :CAP], out_recv[p], preferred_element_type=F32)
        return 0

    lax.fori_loop(0, DEV, collect, 0)

    def wait_total(k, _):
        p = behind(k)
        arrived(rows8(w_all, p), w2_rs, p)
        return 0

    lax.fori_loop(1, DEV, wait_total, 0)
    for r in range(3):
        lanes = slice(r * WIDTH, (r + 1) * WIDTH)
        w_in_out[:, lanes] = w_all[pl.ds(r, DEV, stride=8), :]
        w_rec_out[:, lanes] = w_all[pl.ds(3 + r, DEV, stride=8), :]
    bias_out[...] = w_all[pl.ds(6, 8, stride=8), :]

    def sent(k, _):
        for copy in (ask_copy(k), x_copy(k), agg_copy(k), part_copy(k), out_copy(k), total_copy(k)):
            copy.wait_send()
        return 0

    lax.fori_loop(1, DEV, sent, 0)


def per_device(link_ids, path_states, final_grad, link_states, agg_grad, w_in, w_rec, b_in, b_rec):
    vmem = pl.BlockSpec(memory_space=pltpu.VMEM)
    dma = pltpu.SemaphoreType.DMA((DEV,))
    rows_pair = pltpu.VMEM((DEV, CAP, WIDTH), BF16)
    wide = pltpu.VMEM((ROWS, WIDTH), F32)
    path_grad, link_grad, w_in_grad, w_rec_grad, bias = pl.pallas_call(
        kernel,
        out_shape=(
            jax.ShapeDtypeStruct((PATHS, WIDTH), BF16),
            jax.ShapeDtypeStruct((LINKS, WIDTH), F32),
            jax.ShapeDtypeStruct((WIDTH, 3 * WIDTH), F32),
            jax.ShapeDtypeStruct((WIDTH, 3 * WIDTH), F32),
            jax.ShapeDtypeStruct((8, WIDTH), F32),
        ),
        in_specs=[vmem] * 9,
        out_specs=(vmem,) * 5,
        scratch_shapes=[
            pltpu.VMEM((PATHS, PATHS), BF16),
            pltpu.VMEM((HOPS, PATHS), I32),
            pltpu.VMEM((HOPS, PATHS), I32),
            pltpu.VMEM((DEV, 512), F32),
            pltpu.VMEM((DEV, 1, 128), I32),
            pltpu.VMEM((DEV, 1, 128), I32),
            pltpu.VMEM((128, DEV), F32),
            pltpu.VMEM((DEV, 128), I32),
            pltpu.SMEM((HOPS, PATHS), I32),
            pltpu.SMEM((DEV, 128), I32),
            pltpu.VMEM((LINKS, 2 * WIDTH), BF16),
            rows_pair, rows_pair, rows_pair, rows_pair, rows_pair, rows_pair,
            pltpu.VMEM((DEV * CAP, WIDTH), F32),
            pltpu.VMEM((ROWS + 8, WIDTH), F32),
            pltpu.VMEM((PATHS, WIDTH), F32),
            wide, wide, wide, wide, wide,
            pltpu.VMEM((ROWS, WIDTH), BF16),
            pltpu.VMEM((ROWS, WIDTH), BF16),
            pltpu.VMEM((PATHS, WIDTH), F32),
            pltpu.VMEM((DEV * 8 + 8, WIDTH), F32),
            pltpu.VMEM((DEV * 8 + 8, WIDTH), F32),
            pltpu.VMEM((8, WIDTH), F32),
            pltpu.VMEM((DEV * 8 + 8, WIDTH), F32),
            pltpu.VMEM((8, 3 * WIDTH), F32),
        ] + [dma] * 12 + [pltpu.SemaphoreType.DMA((2,))],
        compiler_params=pltpu.CompilerParams(
            collective_id=0, has_side_effects=True, vmem_limit_bytes=60 * 2**20
        ),
    )(
        jnp.transpose(link_ids), path_states, final_grad, link_states, agg_grad, w_in, w_rec,
        b_in.reshape(1, 3 * WIDTH), b_rec.reshape(1, 3 * WIDTH),
    )
    return (
        path_grad, link_grad, w_in_grad, w_rec_grad,
        bias[:3].reshape(3 * WIDTH), bias[3:6].reshape(3 * WIDTH),
    )


def solution(mesh):
    rows = P(("outer", "grp"), None)
    return jax.shard_map(
        per_device,
        mesh=mesh,
        in_specs=(rows, P(("outer", "grp"), None, None), rows, rows, rows, P(), P(), P(), P()),
        out_specs=(rows, rows, P(), P(), P(), P()),
        check_vma=False,
    )
```

time: 610 us -> 216 us (0.35)
  the two profiles are of different devices: /device:TPU:1 before, /device:TPU:56 now
where the time goes in v1:
time: 216 us
  Pallas kernels  205 us (95%)
  local copies, waits for them, and re-layouts  9.5 us (4%)
    pallas_call x1, Pallas kernels, per_device(): pl.pallas_call(kernel, out_shape=(jax.ShapeDtypeStruct((PATHS, WIDTH), BF...  205 us
    unnamed x6, local copies, waits for them, and re-layouts  5.68 us

profile of v1, /device:TPU:56, one launch (start us, length us, event | category | flops | bytes accessed | tf_op | source)
XLA Modules:
  0.0 215.5 jit_solution(7073053716801291252)
XLA Ops:
  0.6 1.2 reshape.24.b_in_ref
  1.9 1.2 reshape.25.b_rec_ref
  3.1 205.3 %shard_map.136 = (bf16[768,128]{1,0:T(8,128)(2,1)}, f32[768,128]{1,0:T(8,128)}, f32[128,384]{1,0:T(8,128)}, f32[128,384]{1,0:T(8,128)}, f32[8,128]{1,0:T(8,128)}) custom-call(s32[8,768]{1,0:T(8,128)} %bitcast.5, bf16[768,8,128]{2,1,0:T(8,128)(2,1)} %states_ref.1, bf16[768,128]{1,0:T(8,128)(2,1)} %final_ref.1, bf16[768,128]{1,0:T(8,128)(2,1)} %link_ref.1, ...), custom_call_target="tpu_custom_call" | custom-call | tf_op jit(solution)/shard_map/pallas_call | solution.py:386
  208.5 0.0 copy-start
  208.5 1.3 slice_bitcast_fusion
  209.8 1.6 copy.19
  211.4 1.8 copy.20
  213.2 1.6 copy.21
  214.8 0.0 copy-done
  214.8 0.7 copy.22
Async XLA Ops:
  208.5 6.3 %copy-start = (f32[128,384]{1,0:T(8,128)S(1)}, f32[128,384]{1,0:T(8,128)}, u32[]{:S(2)}) copy-start(f32[128,384]{1,0:T(8,128)} %get-tuple-element.27) | copy-start | bytes 589828

commit v2 on v1

v2 whole, which is shorter than its diff:
```python
import functools
import math

import jax
import jax.numpy as jnp
from jax import lax
from jax.experimental import pallas as pl
from jax.experimental.pallas import tpu as pltpu
from jax.sharding import PartitionSpec as P

MESH = pl.DeviceIdType.MESH
F32 = jnp.float32
BF16 = jnp.bfloat16
I32 = jnp.int32

OUTER = 32
GRP = 4
DEV = OUTER * GRP
HOPS = 8
PATHS = 768
LINKS = 768
WIDTH = 128
ROWS = PATHS * HOPS
CAP = 3 * ROWS // (2 * DEV)
STRIDE = 11
CHUNK = 256
NT = (((1,), (1,)), ((), ()))
TN = (((0,), (0,)), ((), ()))


def iota(shape, dim):
    return lax.broadcasted_iota(I32, shape, dim)


def kernel(
    ids_ref, states_ref, final_ref, link_ref, agg_ref, w_in_ref, w_rec_ref, b_in_ref, b_rec_ref,
    path_out, link_out, w_in_out, w_rec_out, bias_out,
    upper, owner_v, slot_v, asks, ask_rows, pos_rows, ask_send, ask_recv, ask_cols, pos_v, slot_s, pos_s, table,
    x_send, agg_send, x_recv, agg_recv, out_send, out_recv, rows_f, states_f, stage,
    coef_a, coef_b, coef_g, coef_r, coef_u, xh, pre, carry, w_big, w_sum, w_part, w_pair, w_recv, w_total, w_all,
    ask_ss, ask_rs, x_ss, x_rs, agg_ss, agg_rs, out_ss, out_rs, w1_ss, w1_rs, w2_ss, w2_rs, pair_s, local_s,
):
    me_o = lax.axis_index("outer")
    me_g = lax.axis_index("grp")
    me = me_o * GRP + me_g

    grps = [lax.rem(me_g + q, GRP) for q in range(GRP)]

    def ahead(i):
        return lax.rem(me_o + lax.rem(i * STRIDE, OUTER), OUTER)

    def behind(i):
        return lax.rem(me_o + OUTER - lax.rem(i * STRIDE, OUTER), OUTER)

    def to_others(act):
        for q in range(1, GRP):
            act(me_o, grps[q])

        def body(i, _):
            o = ahead(i)
            for q in range(GRP):
                act(o, grps[q])
            return 0

        lax.fori_loop(1, OUTER, body, 0)

    def send(src, dst, send_sem, recv_sem, o, g):
        pltpu.make_async_remote_copy(
            src_ref=src, dst_ref=dst, send_sem=send_sem, recv_sem=recv_sem,
            device_id=(o, g), device_id_type=MESH,
        ).start()

    def done(ref, sem):
        pltpu.make_async_copy(ref, ref, sem).wait()

    barrier = pltpu.get_barrier_semaphore()
    to_others(
        lambda o, g: pl.semaphore_signal(barrier, inc=1, device_id=(o, g), device_id_type=MESH)
    )

    def upper_block(b, _):
        r = pl.multiple_of(b * 128, 128)
        upper[pl.ds(r, 128), :] = jnp.where(
            iota((128, PATHS), 0) + r < iota((128, PATHS), 1), 1.0, 0.0
        ).astype(BF16)
        return 0

    lax.fori_loop(0, PATHS // 128, upper_block, 0)
    owner_v[...] = ((ids_ref[...] >> 8) * 171) >> 9
    asks[...] = jnp.zeros_like(asks)

    def index_hop(t, base):
        own = owner_v[pl.ds(t, 1), :]
        local = ids_ref[pl.ds(t, 1), :] - own * LINKS + 1
        hot = iota((DEV, PATHS), 0) == own
        hot_b = jnp.where(hot, 1.0, 0.0).astype(BF16)
        before = jnp.dot(hot_b, upper[...], preferred_element_type=F32) + base
        rank = jnp.sum(jnp.where(hot, before, 0.0), axis=0, keepdims=True).astype(I32)
        slot = jnp.clip(own * CAP + rank, 0, DEV * CAP - 1)
        slot_v[pl.ds(pl.multiple_of(t * PATHS, PATHS), PATHS)] = slot.reshape(PATHS)
        at_rank = iota((128, PATHS), 0) == rank
        pos = iota((1, PATHS), 1) + t * PATHS

        def parts(row, bits):
            high = (row >> bits).astype(F32)
            low = (row & ((1 << bits) - 1)).astype(F32)
            both = jnp.concatenate(
                [jnp.where(at_rank, high, 0.0), jnp.where(at_rank, low, 0.0)], axis=0
            ).astype(BF16)
            return lax.dot_general(hot_b, both, NT, preferred_element_type=F32)

        asks[:, :256] += parts(local, 5)
        asks[:, 256:] += parts(pos, 7)
        return base + jnp.sum(jnp.where(hot, 1.0, 0.0), axis=1, keepdims=True)

    lax.fori_loop(0, HOPS, index_hop, jnp.zeros((DEV, 1), F32))
    ask_rows[...] = (asks[:, :128] * 32.0 + asks[:, 128:256]).astype(I32)
    pos = (asks[:, 256:384] * 128.0 + asks[:, 384:]).astype(I32)
    pos_rows[...] = jnp.clip(pos, 0, ROWS - 1)

    def spread(o, _):
        ask_send[o] = ask_rows[pl.ds(o, 1), :]
        pos = pos_rows[pl.ds(o, 1), :]
        pos_v[pl.ds(pl.multiple_of(o * 128, 128), 128)] = pos.reshape(128)
        return 0

    lax.fori_loop(0, DEV, spread, 0)
    to_slots = pltpu.make_async_copy(slot_v, slot_s, local_s.at[0])
    to_pos = pltpu.make_async_copy(pos_v, pos_s, local_s.at[1])
    to_slots.start()
    to_pos.start()

    ask_recv[me] = ask_send[me]
    pl.semaphore_wait(barrier, DEV - 1)

    to_others(
        lambda o, g: send(ask_send.at[o * GRP + g], ask_recv.at[me], ask_ss, ask_rs, o, g)
    )

    table[:, :WIDTH] = link_ref[...]
    table[:, WIDTH:] = agg_ref[...]

    def widen(b, _):
        r = pl.multiple_of(b * 64, 64)
        block = states_ref[pl.ds(r, 64)].astype(F32)
        states_f[pl.ds(pl.multiple_of(b * 512, 512), 512), :] = block.reshape(512, WIDTH)
        return 0

    lax.fori_loop(0, PATHS // 64, widen, 0)
    carry[...] = final_ref[...].astype(F32)
    third = 2 * WIDTH
    none = jnp.zeros((WIDTH, WIDTH), BF16)
    w_big[:WIDTH, : 3 * WIDTH] = w_in_ref[...]
    w_big[:WIDTH, 3 * WIDTH :] = none
    w_big[WIDTH:, :third] = w_rec_ref[:, :third]
    w_big[WIDTH:, third : 3 * WIDTH] = none
    w_big[WIDTH:, 3 * WIDTH :] = w_rec_ref[:, third:]
    b_in = b_in_ref[...].reshape(1, 3 * WIDTH)
    b_rec = b_rec_ref[...].reshape(1, 3 * WIDTH)
    bias = jnp.concatenate(
        [b_in[:, :third] + b_rec[:, :third], b_in[:, third:], b_rec[:, third:]], axis=1
    )
    to_slots.wait()
    to_pos.wait()

    done(ask_recv.at[pl.ds(0, DEV - 1)], ask_rs)
    ask_cols[...] = jnp.transpose((ask_recv[...].reshape(DEV, 128) - 1).astype(F32))

    def answer(i, first):
        o = ahead(i)
        cols = []
        for g in range(GRP):
            mine = jnp.where(iota((CAP, 128), 1) == o * GRP + g, ask_cols[:CAP, :], 0.0)
            cols.append(jnp.sum(mine, axis=1, keepdims=True))
        col = jnp.concatenate(cols, axis=0).astype(I32)
        hot = jnp.where(iota((GRP * CAP, LINKS), 1) == col, 1.0, 0.0).astype(BF16)
        got = jnp.dot(hot, table[...], preferred_element_type=F32)
        for g in range(GRP):
            x_send[o * GRP + g] = got[g * CAP : (g + 1) * CAP, :WIDTH].astype(BF16)
            agg_send[o * GRP + g] = got[g * CAP : (g + 1) * CAP, WIDTH:].astype(BF16)
        for q in range(first, GRP):
            p = o * GRP + grps[q]
            send(x_send.at[p], x_recv.at[me], x_ss, x_rs.at[me_o], o, grps[q])
        return 0

    answer(0, 1)
    lax.fori_loop(1, OUTER, lambda i, _: answer(i, 0), 0)
    x_recv[me] = x_send[me]
    agg_recv[me] = agg_send[me]

    def send_agg(o, first):
        for q in range(first, GRP):
            p = o * GRP + grps[q]
            send(agg_send.at[p], agg_recv.at[me], agg_ss, agg_rs.at[me_o], o, grps[q])

    def take(recv, recv_sem, then):
        def rows_of(o):
            block = recv[pl.ds(o * GRP, GRP)].astype(F32).reshape(GRP * CAP, WIDTH)
            rows_f[pl.ds(pl.multiple_of(o * GRP * CAP, 8), GRP * CAP), :] = block

        done(recv.at[pl.ds(0, GRP - 1)], recv_sem.at[me_o])
        rows_of(me_o)
        then(me_o, 1)

        def body(i, _):
            o = behind(i)
            done(recv.at[pl.ds(o * GRP, GRP)], recv_sem.at[o])
            then(ahead(i), 0)
            rows_of(o)
            return 0

        lax.fori_loop(1, OUTER, body, 0)

    def to_path_order(t):
        def body(b, _):
            r = pl.multiple_of(b * 32, 32)
            got = [rows_f[pl.ds(slot_s[t * PATHS + r + j], 1), :] for j in range(32)]
            for j in range(32):
                stage[pl.ds(r + j, 1), :] = got[j]
            return 0

        lax.fori_loop(0, PATHS // 32, body, 0)

    take(x_recv, x_rs, send_agg)

    def forward_hop(t, _):
        to_path_order(t)

        def chunk(c, _):
            r = pl.multiple_of(c * CHUNK, CHUNK)
            out = pl.ds(pl.multiple_of(t * PATHS + r, CHUNK), CHUNK)
            h = states_f[pl.ds(r * HOPS + t, CHUNK, stride=HOPS), :]
            xh[out, :WIDTH] = stage[pl.ds(r, CHUNK), :].astype(BF16)
            xh[out, WIDTH:] = h.astype(BF16)
            both = jnp.dot(xh[out, :], w_big[...], preferred_element_type=F32) + bias
            u = jax.nn.sigmoid(both[:, :WIDTH])
            r_gate = jax.nn.sigmoid(both[:, WIDTH : 2 * WIDTH])
            recur = both[:, 3 * WIDTH :]
            cand = jnp.tanh(both[:, 2 * WIDTH : 3 * WIDTH] + r_gate * recur)
            coef_a[out, :] = (1.0 - u) * (1.0 - cand * cand)
            coef_b[out, :] = (h - cand) * u * (1.0 - u)
            coef_g[out, :] = recur * r_gate * (1.0 - r_gate)
            coef_r[out, :] = r_gate
            coef_u[out, :] = u
            return 0

        lax.fori_loop(0, PATHS // CHUNK, chunk, 0)
        return 0

    lax.fori_loop(0, HOPS, forward_hop, 0)
    take(agg_recv, agg_rs, lambda o, first: None)
    grads = coef_a

    def backward_hop(i, _):
        t = HOPS - 1 - i
        to_path_order(t)

        def chunk(c, _):
            r = pl.multiple_of(c * CHUNK, CHUNK)
            here = pl.ds(r, CHUNK)
            out = pl.ds(pl.multiple_of(t * PATHS + r, CHUNK), CHUNK)
            cg = carry[here, :] + stage[here, :]
            pc = cg * coef_a[out, :]
            parts = [cg * coef_b[out, :], pc * coef_g[out, :], pc, pc * coef_r[out, :]]
            rounded = jnp.concatenate([part.astype(BF16) for part in parts], axis=1)
            pre[out, :] = rounded
            back = lax.dot_general(rounded, w_big[...], NT, preferred_element_type=F32)
            grads[out, :] = back[:, :WIDTH]
            carry[here, :] = cg * coef_u[out, :] + back[:, WIDTH:]
            return 0

        lax.fori_loop(0, PATHS // CHUNK, chunk, 0)
        return 0

    lax.fori_loop(0, HOPS, backward_hop, 0)

    def give(o, g):
        p = o * GRP + g
        for first in range(0, CAP, 24):
            got = [grads[pl.ds(pos_s[p * 128 + first + j], 1), :] for j in range(24)]
            for j in range(24):
                stage[pl.ds(first + j, 1), :] = got[j]
        out_send[p] = stage[:CAP, :].astype(BF16)

    def give_group(i, _):
        o = ahead(i)
        for q in range(GRP):
            give(o, grps[q])
            send(out_send.at[o * GRP + grps[q]], out_recv.at[me], out_ss, out_rs.at[me_o], o, grps[q])
        return 0

    def rows8(ref, n):
        return ref.at[pl.ds(pl.multiple_of(n * 8, 8), 8), :]

    core = lax.rem(me_o, 2)
    chip = me_o // 2
    seat = chip * GRP + me_g
    half = DEV // 2
    mine = pl.ds(pl.multiple_of(core * half * 8, 8), half * 8)
    theirs = pl.ds(pl.multiple_of((1 - core) * half * 8, 8), half * 8)
    twin = me_o + 1 - 2 * core

    def to_same_core(act):
        for q in range(1, GRP):
            act(chip, grps[q])

        def body(i, _):
            z = lax.rem(chip + lax.rem(i * 5, OUTER // 2), OUTER // 2)
            for q in range(GRP):
                act(z, grps[q])
            return 0

        lax.fori_loop(1, OUTER // 2, body, 0)

    lax.fori_loop(1, 6, give_group, 0)
    w_sum[...] = jnp.zeros_like(w_sum)

    def weights(c, sums):
        rows = pl.ds(pl.multiple_of(c * PATHS, PATHS), PATHS)
        w_sum[...] += lax.dot_general(xh[rows, :], pre[rows, :], TN, preferred_element_type=F32)
        return sums + jnp.sum(pre[rows, :].astype(F32), axis=0, keepdims=True)

    sums = lax.fori_loop(0, HOPS, weights, jnp.zeros((1, 4 * WIDTH), F32))

    w_rows = [w_sum[:WIDTH, r * WIDTH : (r + 1) * WIDTH] for r in (0, 1, 2)]
    w_rows += [w_sum[WIDTH:, r * WIDTH : (r + 1) * WIDTH] for r in (0, 1, 3)]
    for r in range(6):
        w_part[pl.ds(r, DEV, stride=8), :] = w_rows[r]
    bias8 = jnp.concatenate(
        [sums[:, r * WIDTH : (r + 1) * WIDTH] for r in (0, 1, 2, 0, 1, 3)]
        + [jnp.zeros((2, WIDTH), F32)],
        axis=0,
    )
    w_part[pl.ds(6, DEV, stride=8), :] = jnp.concatenate([bias8] * (DEV // 8), axis=0)
    w_part[pl.ds(7, DEV, stride=8), :] = jnp.zeros((DEV, WIDTH), F32)
    send(w_part.at[theirs, :], w_pair, pair_s.at[0], pair_s.at[1], twin, me_g)
    lax.fori_loop(6, 14, give_group, 0)
    done(w_pair, pair_s.at[1])
    w_pair[...] += w_part[mine, :]
    to_same_core(
        lambda z, g: send(
            rows8(w_pair, z * GRP + g), rows8(w_recv, seat), w1_ss, w1_rs, z * 2 + core, g
        )
    )
    lax.fori_loop(14, 26, give_group, 0)
    done(w_recv.at[pl.ds(0, (half - 1) * 8)], w1_rs)
    own_rows = pl.ds(pl.multiple_of(seat * 8, 8), 8)
    w_recv[own_rows, :] = w_pair[own_rows, :]
    total = jnp.sum(w_recv[...].reshape(half, 8, WIDTH), axis=0)
    total = total * (1.0 / math.sqrt(ROWS * DEV))
    w_total[...] = total
    line = core * half + seat
    to_same_core(
        lambda z, g: send(w_total, rows8(w_all, line), w2_ss, w2_rs, z * 2 + core, g)
    )
    w_all[pl.ds(pl.multiple_of(line * 8, 8), 8), :] = total
    lax.fori_loop(26, OUTER, give_group, 0)
    for q in range(1, GRP):
        give(me_o, grps[q])
        send(out_send.at[me_o * GRP + grps[q]], out_recv.at[me], out_ss, out_rs.at[me_o], me_o, grps[q])
    give(me_o, me_g)
    out_recv[me] = out_send[me]
    path_out[...] = carry[...].astype(BF16)

    link_out[...] = jnp.zeros_like(link_out)

    def collect(o):
        part = jnp.zeros((LINKS, WIDTH), F32)
        for g in range(GRP):
            p = o * GRP + g
            hot = jnp.where(iota((LINKS, 128), 0) == ask_recv[p] - 1, 1.0, 0.0).astype(BF16)
            part += jnp.dot(hot[:, :CAP], out_recv[p], preferred_element_type=F32)
        link_out[...] += part

    def collect_next(i, _):
        o = behind(i)
        done(out_recv.at[pl.ds(o * GRP, GRP)], out_rs.at[o])
        collect(o)
        return 0

    lax.fori_loop(1, OUTER // 2, collect_next, 0)
    done(w_all.at[pl.ds(0, (half - 1) * 8)], w2_rs)
    send(w_all.at[mine, :], w_all.at[mine, :], pair_s.at[2], pair_s.at[3], twin, me_g)
    lax.fori_loop(OUTER // 2, OUTER, collect_next, 0)
    done(out_recv.at[pl.ds(0, GRP - 1)], out_rs.at[me_o])
    collect(me_o)
    done(w_all.at[theirs, :], pair_s.at[3])
    for r in range(3):
        lanes = slice(r * WIDTH, (r + 1) * WIDTH)
        w_in_out[:, lanes] = w_all[pl.ds(r, DEV, stride=8), :]
        w_rec_out[:, lanes] = w_all[pl.ds(3 + r, DEV, stride=8), :]
    bias_out[...] = w_all[pl.ds(6, 8, stride=8), :]

    for buf, sem in (
        (ask_send, ask_ss), (x_send, x_ss), (agg_send, agg_ss), (out_send, out_ss)
    ):
        done(buf.at[pl.ds(0, DEV - 1)], sem)
    done(w_recv.at[pl.ds(0, (half - 1) * 8)], w1_ss)
    done(w_recv.at[pl.ds(0, (half - 1) * 8)], w2_ss)
    done(w_pair, pair_s.at[0])
    done(w_pair, pair_s.at[2])


def finish(path, link, w_in, w_rec, bias, path_out, link_out, w_in_out, w_rec_out, b_in_out, b_rec_out):
    path_out[...] = path[...]
    link_out[...] = link[...]
    w_in_out[...] = w_in[...]
    w_rec_out[...] = w_rec[...]
    for r in range(3):
        b_in_out[pl.ds(r * WIDTH, WIDTH)] = bias[r, :]
        b_rec_out[pl.ds(r * WIDTH, WIDTH)] = bias[3 + r, :]


def per_device(link_ids, path_states, final_grad, link_states, agg_grad, w_in, w_rec, b_in, b_rec):
    vmem = pl.BlockSpec(memory_space=pltpu.VMEM)
    one = pltpu.SemaphoreType.DMA
    some = pltpu.SemaphoreType.DMA((OUTER,))
    rows_pair = pltpu.VMEM((DEV, CAP, WIDTH), BF16)
    wide = pltpu.VMEM((ROWS, WIDTH), F32)
    shapes = (
        jax.ShapeDtypeStruct((PATHS, WIDTH), BF16),
        jax.ShapeDtypeStruct((LINKS, WIDTH), F32),
        jax.ShapeDtypeStruct((WIDTH, 3 * WIDTH), F32),
        jax.ShapeDtypeStruct((WIDTH, 3 * WIDTH), F32),
    )
    results = pl.pallas_call(
        kernel,
        out_shape=shapes + (jax.ShapeDtypeStruct((8, WIDTH), F32),),
        in_specs=[vmem] * 9,
        out_specs=(vmem,) * 5,
        scratch_shapes=[
            pltpu.VMEM((PATHS, PATHS), BF16),
            pltpu.VMEM((HOPS, PATHS), I32),
            pltpu.VMEM((ROWS,), I32),
            pltpu.VMEM((DEV, 512), F32),
            pltpu.VMEM((DEV, 128), I32),
            pltpu.VMEM((DEV, 128), I32),
            pltpu.VMEM((DEV, 1, 128), I32),
            pltpu.VMEM((DEV, 1, 128), I32),
            pltpu.VMEM((128, DEV), F32),
            pltpu.VMEM((DEV * 128,), I32),
            pltpu.SMEM((ROWS,), I32),
            pltpu.SMEM((DEV * 128,), I32),
            pltpu.VMEM((LINKS, 2 * WIDTH), BF16),
            rows_pair, rows_pair, rows_pair, rows_pair, rows_pair, rows_pair,
            pltpu.VMEM((DEV * CAP, WIDTH), F32),
            pltpu.VMEM((ROWS + 8, WIDTH), F32),
            pltpu.VMEM((PATHS, WIDTH), F32),
            wide, wide, wide, wide, wide,
            pltpu.VMEM((ROWS, 2 * WIDTH), BF16),
            pltpu.VMEM((ROWS, 4 * WIDTH), BF16),
            pltpu.VMEM((PATHS, WIDTH), F32),
            pltpu.VMEM((2 * WIDTH, 4 * WIDTH), BF16),
            pltpu.VMEM((2 * WIDTH, 4 * WIDTH), F32),
            pltpu.VMEM((DEV * 8 + 8, WIDTH), F32),
            pltpu.VMEM((DEV * 4, WIDTH), F32),
            pltpu.VMEM((DEV * 4, WIDTH), F32),
            pltpu.VMEM((8, WIDTH), F32),
            pltpu.VMEM((DEV * 8 + 8, WIDTH), F32),
        ] + [one, one, one, some, one, some, one, some, one, one, one, one]
        + [pltpu.SemaphoreType.DMA((4,)), pltpu.SemaphoreType.DMA((2,))],
        compiler_params=pltpu.CompilerParams(
            collective_id=0, has_side_effects=True, vmem_limit_bytes=60 * 2**20
        ),
    )(
        jnp.transpose(link_ids), path_states, final_grad, link_states, agg_grad, w_in, w_rec,
        b_in, b_rec,
    )
    flat = jax.ShapeDtypeStruct((3 * WIDTH,), F32)
    return pl.pallas_call(
        finish,
        out_shape=shapes + (flat, flat),
        in_specs=[vmem] * 5,
        out_specs=(vmem,) * 6,
    )(*results)


def solution(mesh):
    rows = P(("outer", "grp"), None)
    return jax.shard_map(
        per_device,
        mesh=mesh,
        in_specs=(rows, P(("outer", "grp"), None, None), rows, rows, rows, P(), P(), P(), P()),
        out_specs=(rows, rows, P(), P(), P(), P()),
        check_vma=False,
    )
```

time: 216 us -> 142 us (0.66)
  the two profiles are of different devices: /device:TPU:56 before, /device:TPU:1 now
where the time goes in v2:
time: 142 us
  Pallas kernels  141 us (99%)
    pallas_call x1, Pallas kernels, per_device(): pl.pallas_call(kernel, out_shape=shapes + (jax.ShapeDtypeStruct((8, WIDTH...  139 us

profile of v2, /device:TPU:1, one launch (start us, length us, event | category | flops | bytes accessed | tf_op | source)
XLA Modules:
  0.0 141.5 jit_solution(1238179774938393049)
XLA Ops:
  0.6 138.7 %shard_map.136 = (bf16[768,128]{1,0:T(8,128)(2,1)}, f32[768,128]{1,0:T(8,128)}, f32[128,384]{1,0:T(8,128)}, f32[128,384]{1,0:T(8,128)}, f32[8,128]{1,0:T(8,128)}) custom-call(s32[8,768]{1,0:T(8,128)} %bitcast.1, bf16[768,8,128]{2,1,0:T(8,128)(2,1)} %states_ref.1, bf16[768,128]{1,0:T(8,128)(2,1)} %final_ref.1, bf16[768,128]{1,0:T(8,128)(2,1)} %link_ref.1, ...), custom_call_target="tpu_custom_call" | custom-call | tf_op jit(solution)/shard_map/pallas_call | solution.py:426
  139.4 2.2 %shard_map.137 = (bf16[768,128]{1,0:T(8,128)(2,1)}, f32[768,128]{1,0:T(8,128)}, f32[128,384]{1,0:T(8,128)}, f32[128,384]{1,0:T(8,128)}, f32[384]{0:T(512)}, /*index=5*/f32[384]{0:T(512)}) custom-call(bf16[768,128]{1,0:T(8,128)(2,1)} %get-tuple-element.11.path, f32[768,128]{1,0:T(8,128)} %get-tuple-element.12.link, f32[128,384]{1,0:T(8,128)} %get-tuple-element.13.w_in, ...), custom_call_target="tpu_custom_call" | custom-call | tf_op jit(solution)/shard_map/pallas_call | solution.py:470

commit v3 on v2

--- a/solution.py
+++ b/solution.py
@@ -23,7 +23,7 @@
 ROWS = PATHS * HOPS
 CAP = 3 * ROWS // (2 * DEV)
 STRIDE = 11
-CHUNK = 256
+CHUNK = 768
 NT = (((1,), (1,)), ((), ()))
 TN = (((0,), (0,)), ((), ()))
 
@@ -193,23 +193,12 @@
             p = o * GRP + grps[q]
             send(agg_send.at[p], agg_recv.at[me], agg_ss, agg_rs.at[me_o], o, grps[q])
 
-    def take(recv, recv_sem, then):
-        def rows_of(o):
-            block = recv[pl.ds(o * GRP, GRP)].astype(F32).reshape(GRP * CAP, WIDTH)
-            rows_f[pl.ds(pl.multiple_of(o * GRP * CAP, 8), GRP * CAP), :] = block
-
-        done(recv.at[pl.ds(0, GRP - 1)], recv_sem.at[me_o])
-        rows_of(me_o)
-        then(me_o, 1)
-
-        def body(i, _):
-            o = behind(i)
-            done(recv.at[pl.ds(o * GRP, GRP)], recv_sem.at[o])
-            then(ahead(i), 0)
-            rows_of(o)
-            return 0
-
-        lax.fori_loop(1, OUTER, body, 0)
+    def take(recv, recv_sem, i, own=False):
+        o = me_o if own else behind(i)
+        done(recv.at[pl.ds(o * GRP, GRP - 1 if own else GRP)], recv_sem.at[o])
+        block = recv[pl.ds(o * GRP, GRP)].astype(F32).reshape(GRP * CAP, WIDTH)
+        rows_f[pl.ds(pl.multiple_of(o * GRP * CAP, 8), GRP * CAP), :] = block
+        return 0
 
     def to_path_order(t):
         def body(b, _):
@@ -221,7 +210,19 @@
 
         lax.fori_loop(0, PATHS // 32, body, 0)
 
-    take(x_recv, x_rs, send_agg)
+    half_way = OUTER // 2 + 1
+
+    def take_and_send(i, _):
+        take(x_recv, x_rs, i)
+        send_agg(ahead(2 * (i - half_way) + 1), 0)
+        send_agg(ahead(2 * (i - half_way) + 2), 0)
+        return 0
+
+    take(x_recv, x_rs, 0, own=True)
+    lax.fori_loop(1, half_way, lambda i, _: take(x_recv, x_rs, i), 0)
+    send_agg(me_o, 1)
+    send_agg(ahead(OUTER - 1), 0)
+    lax.fori_loop(half_way, OUTER, take_and_send, 0)
 
     def forward_hop(t, _):
         to_path_order(t)
@@ -248,7 +249,8 @@
         return 0
 
     lax.fori_loop(0, HOPS, forward_hop, 0)
-    take(agg_recv, agg_rs, lambda o, first: None)
+    take(agg_recv, agg_rs, 0, own=True)
+    lax.fori_loop(1, OUTER, lambda i, _: take(agg_recv, agg_rs, i), 0)
     grads = coef_a
 
     def backward_hop(i, _):

time: 142 us -> 139 us (0.979)
  Pallas kernels: 141 us -> 137 us
    pallas_call x1, Pallas kernels: 139 us -> 135 us  [per_device(): pl.pallas_call(kernel, out_shape=shapes + (jax.ShapeDtypeStruct((8, WIDTH...]
where the time goes in v3:
time: 139 us; the launch traced here: 138 us
  Pallas kernels  137 us (99%)
    pallas_call x1, Pallas kernels, per_device(): pl.pallas_call(kernel, out_shape=shapes + (jax.ShapeDtypeStruct((8, WIDTH...  135 us

profile of v3, /device:TPU:1, one launch (start us, length us, event | category | flops | bytes accessed | tf_op | source)
XLA Modules:
  0.0 138.1 jit_solution(8013497812459161280)
XLA Ops:
  0.6 135.3 %shard_map.136 = (bf16[768,128]{1,0:T(8,128)(2,1)}, f32[768,128]{1,0:T(8,128)}, f32[128,384]{1,0:T(8,128)}, f32[128,384]{1,0:T(8,128)}, f32[8,128]{1,0:T(8,128)}) custom-call(s32[8,768]{1,0:T(8,128)} %bitcast.1, bf16[768,8,128]{2,1,0:T(8,128)(2,1)} %states_ref.1, bf16[768,128]{1,0:T(8,128)(2,1)} %final_ref.1, bf16[768,128]{1,0:T(8,128)(2,1)} %link_ref.1, ...), custom_call_target="tpu_custom_call" | custom-call | tf_op jit(solution)/shard_map/pallas_call | solution.py:428
  135.9 2.2 %shard_map.137 = (bf16[768,128]{1,0:T(8,128)(2,1)}, f32[768,128]{1,0:T(8,128)}, f32[128,384]{1,0:T(8,128)}, f32[128,384]{1,0:T(8,128)}, f32[384]{0:T(512)}, /*index=5*/f32[384]{0:T(512)}) custom-call(bf16[768,128]{1,0:T(8,128)(2,1)} %get-tuple-element.11.path, f32[768,128]{1,0:T(8,128)} %get-tuple-element.12.link, f32[128,384]{1,0:T(8,128)} %get-tuple-element.13.w_in, ...), custom_call_target="tpu_custom_call" | custom-call | tf_op jit(solution)/shard_map/pallas_call | solution.py:472

commit v4 on v3

--- a/solution.py
+++ b/solution.py
@@ -37,7 +37,7 @@
     path_out, link_out, w_in_out, w_rec_out, bias_out,
     upper, owner_v, slot_v, asks, ask_rows, pos_rows, ask_send, ask_recv, ask_cols, pos_v, slot_s, pos_s, table,
     x_send, agg_send, x_recv, agg_recv, out_send, out_recv, rows_f, states_f, stage,
-    coef_a, coef_b, coef_g, coef_r, coef_u, xh, pre, carry, w_big, w_sum, w_part, w_pair, w_recv, w_total, w_all,
+    coef_a, coef_b, coef_g, coef_r, coef_u, xh, pre, carry, w_big, w_sum, w_part, w_pair, w_recv, w_total, w_all, all_b,
     ask_ss, ask_rs, x_ss, x_rs, agg_ss, agg_rs, out_ss, out_rs, w1_ss, w1_rs, w2_ss, w2_rs, pair_s, local_s,
 ):
     me_o = lax.axis_index("outer")
@@ -314,7 +314,7 @@
 
         lax.fori_loop(1, OUTER // 2, body, 0)
 
-    lax.fori_loop(1, 6, give_group, 0)
+    lax.fori_loop(1, 4, give_group, 0)
     w_sum[...] = jnp.zeros_like(w_sum)
 
     def weights(c, sums):
@@ -336,7 +336,7 @@
     w_part[pl.ds(6, DEV, stride=8), :] = jnp.concatenate([bias8] * (DEV // 8), axis=0)
     w_part[pl.ds(7, DEV, stride=8), :] = jnp.zeros((DEV, WIDTH), F32)
     send(w_part.at[theirs, :], w_pair, pair_s.at[0], pair_s.at[1], twin, me_g)
-    lax.fori_loop(6, 14, give_group, 0)
+    lax.fori_loop(4, 7, give_group, 0)
     done(w_pair, pair_s.at[1])
     w_pair[...] += w_part[mine, :]
     to_same_core(
@@ -344,19 +344,19 @@
             rows8(w_pair, z * GRP + g), rows8(w_recv, seat), w1_ss, w1_rs, z * 2 + core, g
         )
     )
-    lax.fori_loop(14, 26, give_group, 0)
+    lax.fori_loop(7, 16, give_group, 0)
     done(w_recv.at[pl.ds(0, (half - 1) * 8)], w1_rs)
     own_rows = pl.ds(pl.multiple_of(seat * 8, 8), 8)
     w_recv[own_rows, :] = w_pair[own_rows, :]
     total = jnp.sum(w_recv[...].reshape(half, 8, WIDTH), axis=0)
     total = total * (1.0 / math.sqrt(ROWS * DEV))
-    w_total[...] = total
+    w_total[...] = total.astype(BF16)
     line = core * half + seat
     to_same_core(
-        lambda z, g: send(w_total, rows8(w_all, line), w2_ss, w2_rs, z * 2 + core, g)
-    )
-    w_all[pl.ds(pl.multiple_of(line * 8, 8), 8), :] = total
-    lax.fori_loop(26, OUTER, give_group, 0)
+        lambda z, g: send(w_total, all_b.at[line], w2_ss, w2_rs, z * 2 + core, g)
+    )
+    all_b[line] = w_total[...]
+    lax.fori_loop(16, OUTER, give_group, 0)
     for q in range(1, GRP):
         give(me_o, grps[q])
         send(out_send.at[me_o * GRP + grps[q]], out_recv.at[me], out_ss, out_rs.at[me_o], me_o, grps[q])
@@ -381,12 +381,13 @@
         return 0
 
     lax.fori_loop(1, OUTER // 2, collect_next, 0)
-    done(w_all.at[pl.ds(0, (half - 1) * 8)], w2_rs)
-    send(w_all.at[mine, :], w_all.at[mine, :], pair_s.at[2], pair_s.at[3], twin, me_g)
+    done(all_b.at[pl.ds(0, half - 1)], w2_rs)
+    send(all_b.at[pl.ds(core * half, half)], all_b.at[pl.ds(core * half, half)], pair_s.at[2], pair_s.at[3], twin, me_g)
     lax.fori_loop(OUTER // 2, OUTER, collect_next, 0)
     done(out_recv.at[pl.ds(0, GRP - 1)], out_rs.at[me_o])
     collect(me_o)
-    done(w_all.at[theirs, :], pair_s.at[3])
+    done(all_b.at[pl.ds((1 - core) * half, half)], pair_s.at[3])
+    w_all[: DEV * 8, :] = all_b[...].astype(F32).reshape(DEV * 8, WIDTH)
     for r in range(3):
         lanes = slice(r * WIDTH, (r + 1) * WIDTH)
         w_in_out[:, lanes] = w_all[pl.ds(r, DEV, stride=8), :]
@@ -398,9 +399,9 @@
     ):
         done(buf.at[pl.ds(0, DEV - 1)], sem)
     done(w_recv.at[pl.ds(0, (half - 1) * 8)], w1_ss)
-    done(w_recv.at[pl.ds(0, (half - 1) * 8)], w2_ss)
+    done(all_b.at[pl.ds(0, half - 1)], w2_ss)
     done(w_pair, pair_s.at[0])
-    done(w_pair, pair_s.at[2])
+    done(all_b.at[pl.ds(0, half)], pair_s.at[2])
 
 
 def finish(path, link, w_in, w_rec, bias, path_out, link_out, w_in_out, w_rec_out, b_in_out, b_rec_out):
@@ -457,8 +458,9 @@
             pltpu.VMEM((DEV * 8 + 8, WIDTH), F32),
             pltpu.VMEM((DEV * 4, WIDTH), F32),
             pltpu.VMEM((DEV * 4, WIDTH), F32),
-            pltpu.VMEM((8, WIDTH), F32),
+            pltpu.VMEM((8, WIDTH), BF16),
             pltpu.VMEM((DEV * 8 + 8, WIDTH), F32),
+            pltpu.VMEM((DEV, 8, WIDTH), BF16),
         ] + [one, one, one, some, one, some, one, some, one, one, one, one]
         + [pltpu.SemaphoreType.DMA((4,)), pltpu.SemaphoreType.DMA((2,))],
         compiler_params=pltpu.CompilerParams(

time: 139 us -> 137 us (0.986)
    pallas_call x1, Pallas kernels: 135 us -> 134 us  [per_device(): pl.pallas_call(kernel, out_shape=shapes + (jax.ShapeDtypeStruct((8, WIDTH...]
where the time goes in v4:
time: 137 us; the launch traced here: 136 us
  Pallas kernels  136 us (99%)
    pallas_call x1, Pallas kernels, per_device(): pl.pallas_call(kernel, out_shape=shapes + (jax.ShapeDtypeStruct((8, WIDTH...  134 us

profile of v4, /device:TPU:1, one launch (start us, length us, event | category | flops | bytes accessed | tf_op | source)
XLA Modules:
  0.0 136.3 jit_solution(13981146058263356255)
XLA Ops:
  0.6 133.5 %shard_map.136 = (bf16[768,128]{1,0:T(8,128)(2,1)}, f32[768,128]{1,0:T(8,128)}, f32[128,384]{1,0:T(8,128)}, f32[128,384]{1,0:T(8,128)}, f32[8,128]{1,0:T(8,128)}) custom-call(s32[8,768]{1,0:T(8,128)} %bitcast.1, bf16[768,8,128]{2,1,0:T(8,128)(2,1)} %states_ref.1, bf16[768,128]{1,0:T(8,128)(2,1)} %final_ref.1, bf16[768,128]{1,0:T(8,128)(2,1)} %link_ref.1, ...), custom_call_target="tpu_custom_call" | custom-call | tf_op jit(solution)/shard_map/pallas_call | solution.py:429
  134.2 2.2 %shard_map.137 = (bf16[768,128]{1,0:T(8,128)(2,1)}, f32[768,128]{1,0:T(8,128)}, f32[128,384]{1,0:T(8,128)}, f32[128,384]{1,0:T(8,128)}, f32[384]{0:T(512)}, /*index=5*/f32[384]{0:T(512)}) custom-call(bf16[768,128]{1,0:T(8,128)(2,1)} %get-tuple-element.11.path, f32[768,128]{1,0:T(8,128)} %get-tuple-element.12.link, f32[128,384]{1,0:T(8,128)} %get-tuple-element.13.w_in, ...), custom_call_target="tpu_custom_call" | custom-call | tf_op jit(solution)/shard_map/pallas_call | solution.py:474

commit v5 on v4

--- a/solution.py
+++ b/solution.py
@@ -202,13 +202,13 @@
 
     def to_path_order(t):
         def body(b, _):
-            r = pl.multiple_of(b * 32, 32)
-            got = [rows_f[pl.ds(slot_s[t * PATHS + r + j], 1), :] for j in range(32)]
-            for j in range(32):
+            r = pl.multiple_of(b * 64, 64)
+            got = [rows_f[pl.ds(slot_s[t * PATHS + r + j], 1), :] for j in range(64)]
+            for j in range(64):
                 stage[pl.ds(r + j, 1), :] = got[j]
             return 0
 
-        lax.fori_loop(0, PATHS // 32, body, 0)
+        lax.fori_loop(0, PATHS // 64, body, 0)
 
     half_way = OUTER // 2 + 1
 

time: 137 us -> 137 us (level)
  no operation moved by 1% of the time
where the time goes in v5:
time: 137 us; the launch traced here: 136 us
  Pallas kernels  135 us (99%)
    pallas_call x1, Pallas kernels, per_device(): pl.pallas_call(kernel, out_shape=shapes + (jax.ShapeDtypeStruct((8, WIDTH...  133 us

profile of v5, /device:TPU:1, one launch (start us, length us, event | category | flops | bytes accessed | tf_op | source)
XLA Modules:
  0.0 135.5 jit_solution(6057756684031790087)
XLA Ops:
  0.6 132.7 %shard_map.136 = (bf16[768,128]{1,0:T(8,128)(2,1)}, f32[768,128]{1,0:T(8,128)}, f32[128,384]{1,0:T(8,128)}, f32[128,384]{1,0:T(8,128)}, f32[8,128]{1,0:T(8,128)}) custom-call(s32[8,768]{1,0:T(8,128)} %bitcast.1, bf16[768,8,128]{2,1,0:T(8,128)(2,1)} %states_ref.1, bf16[768,128]{1,0:T(8,128)(2,1)} %final_ref.1, bf16[768,128]{1,0:T(8,128)(2,1)} %link_ref.1, ...), custom_call_target="tpu_custom_call" | custom-call | tf_op jit(solution)/shard_map/pallas_call | solution.py:429
  133.4 2.2 %shard_map.137 = (bf16[768,128]{1,0:T(8,128)(2,1)}, f32[768,128]{1,0:T(8,128)}, f32[128,384]{1,0:T(8,128)}, f32[128,384]{1,0:T(8,128)}, f32[384]{0:T(512)}, /*index=5*/f32[384]{0:T(512)}) custom-call(bf16[768,128]{1,0:T(8,128)(2,1)} %get-tuple-element.11.path, f32[768,128]{1,0:T(8,128)} %get-tuple-element.12.link, f32[128,384]{1,0:T(8,128)} %get-tuple-element.13.w_in, ...), custom_call_target="tpu_custom_call" | custom-call | tf_op jit(solution)/shard_map/pallas_call | solution.py:474
